TPU v7x, 256 devices: a whole 4x4x8 slice. The times are simulated.
256 devices in a mesh: grp: 8 (over y, core), box: 32 (over z, x).
Axes of the slice: x: 4, y: 4, z: 8, core: 2. Of those that a mesh axis runs over, the one named last changes fastest.
Arguments:
- leaves: bfloat16 [2048, 64, 1024], P(('grp', 'box')), may hold values from -6 to 6
- translate: bfloat16 [12, 2048, 64, 256], P(None, ('grp', 'box')), may hold values from -0.375 to 0.375
- local_links: int32 [12, 2, 2048], P(None, None, ('grp', 'box')), may hold values from 0 to 7
- remote_links: int32 [12, 2, 2048], P(None, None, ('grp', 'box')), may hold values from 0 to 3
Outputs:
- coefficients: bfloat16 [2048, 64, 1024], P(('grp', 'box'))
Inputs may be any that keep to these rules, and one draw needn't show every extreme that they name: `local_links`: places among a device's own 8 nodes. `remote_links`: places among the partner's leading 4 nodes.
All inputs are finite; a program needn't handle non-finite values.
Results may differ from a plain program's by a relative error of at most 0.025.
Values may be sent and summed in bfloat16 or wider, within the bound.
A program may use at most 64 MiB of HBM per device.

v0:
```python
import jax
import jax.numpy as jnp
from jax import lax
from jax.sharding import PartitionSpec as P

SEND = 4


def swapped(value, axis, distance):
    mask = 2**distance
    pairs = [(source, source ^ mask) for source in range(lax.axis_size(axis))]
    return lax.ppermute(value, axis, pairs)


def advance(current, matrices, near_links, far_links, swap_bit):
    partner_rows = swapped(current[:SEND], "box", swap_bit)
    own_rows = jnp.concatenate(
        [jnp.take(current, near_links[0], axis=0), jnp.take(current, near_links[1], axis=0)], axis=1
    )
    far_rows = jnp.concatenate(
        [
            jnp.take(partner_rows, far_links[0], axis=0),
            jnp.take(partner_rows, far_links[1], axis=0),
        ],
        axis=1,
    )
    stacked = jnp.concatenate([own_rows, far_rows], axis=1)
    summed = jnp.einsum("nrk,nkb->nrb", matrices, stacked, preferred_element_type=jnp.float32)
    return summed.astype(jnp.bfloat16)


def switch_groups(current):
    return lax.all_to_all(current, "grp", split_axis=0, concat_axis=0, tiled=True)


def on_device(leaves, translate, local_links, remote_links):
    current = leaves
    box_bits = lax.axis_size("box").bit_length() - 1
    level_count = translate.shape[0]
    half_levels = level_count // 2
    for layer_index in range(level_count):
        if layer_index == half_levels:
            current = switch_groups(current)
        swap_bit = layer_index % half_levels % box_bits
        current = advance(
            current,
            translate[layer_index],
            local_links[layer_index],
            remote_links[layer_index],
            swap_bit,
        )
    return current


def solution(mesh):
    placed = (
        P(("grp", "box"), None, None),
        P(None, ("grp", "box"), None, None),
        P(None, None, ("grp", "box")),
        P(None, None, ("grp", "box")),
    )
    return jax.shard_map(
        on_device,
        mesh=mesh,
        in_specs=placed,
        out_specs=P(("grp", "box"), None, None),
        check_vma=False,
    )
```

profile of v0, /device:TPU:2, one launch (start us, length us, event | category | flops | bytes accessed | tf_op | source)
XLA Modules:
  0.0 296.0 jit_solution(3998791018694485685)
XLA Ops:
  1.2 2.4 collective-permute-start
  5.8 1.6 slice_reduce_fusion.1
  7.4 1.6 slice_reduce_fusion.3
  9.5 1.8 gather_fusion.1
  17.5 2.5 fusion.132
  20.1 2.2 collective-permute-start.1
  24.4 2.4 broadcast_select_fusion.42
  28.0 6.1 %collective-permute-done.1 = bf16[4,64,1024]{2,1,0:T(8,128)(2,1)S(1)} collective-permute-done((bf16[4,64,1024]{2,1,0:T(8,128)(2,1)S(1)}, bf16[4,64,1024]{2,1,0:T(8,128)(2,1)S(1)}, u32[]{:S(2)}, u32[]{:S(2)}) %collective-permute-start.1) | collective-permute-done | bytes 524320 | tf_op jit(solution)/shard_map/ppermute | solution.py:12
  36.7 2.5 fusion.135
  39.2 2.3 collective-permute-start.2
  43.7 2.4 broadcast_select_fusion.38
  47.3 4.3 %collective-permute-done.2 = bf16[4,64,1024]{2,1,0:T(8,128)(2,1)S(1)} collective-permute-done((bf16[4,64,1024]{2,1,0:T(8,128)(2,1)S(1)}, bf16[4,64,1024]{2,1,0:T(8,128)(2,1)S(1)}, u32[]{:S(2)}, u32[]{:S(2)}) %collective-permute-start.2) | collective-permute-done | bytes 524320 | tf_op jit(solution)/shard_map/ppermute | solution.py:12
  54.2 2.5 fusion.138
  56.7 3.4 %collective-permute-start.3 = (bf16[4,64,1024]{2,1,0:T(8,128)(2,1)S(1)}, bf16[4,64,1024]{2,1,0:T(8,128)(2,1)S(1)}, u32[]{:S(2)}, u32[]{:S(2)}) collective-permute-start(bf16[4,64,1024]{2,1,0:T(8,128)(2,1)S(1)} %slice.506), channel_id=1, source_target_pairs={{0,8},{1,9},{2,10},{3,11},{4,12},{5,13},{6,14},{7,15},{8,0},{9,1},... | collective-permute-start | bytes 1572872 | tf_op jit(solution)/shard_map/ppermute | solution.py:12
  62.3 2.4 broadcast_select_fusion.34
  65.9 14.8 %collective-permute-done.3 = bf16[4,64,1024]{2,1,0:T(8,128)(2,1)S(1)} collective-permute-done((bf16[4,64,1024]{2,1,0:T(8,128)(2,1)S(1)}, bf16[4,64,1024]{2,1,0:T(8,128)(2,1)S(1)}, u32[]{:S(2)}, u32[]{:S(2)}) %collective-permute-start.3) | collective-permute-done | bytes 524320 | tf_op jit(solution)/shard_map/ppermute | solution.py:12
  83.3 2.5 fusion.141
  85.8 6.5 %collective-permute-start.4 = (bf16[4,64,1024]{2,1,0:T(8,128)(2,1)S(1)}, bf16[4,64,1024]{2,1,0:T(8,128)(2,1)S(1)}, u32[]{:S(2)}, u32[]{:S(2)}) collective-permute-start(bf16[4,64,1024]{2,1,0:T(8,128)(2,1)S(1)} %slice.507), channel_id=1, source_target_pairs={{0,16},{1,17},{2,18},{3,19},{4,20},{5,21},{6,22},{7,23},{8,24},{9,... | collective-permute-start | bytes 1572872 | tf_op jit(solution)/shard_map/ppermute | solution.py:12
  94.5 2.4 broadcast_select_fusion.30
  98.0 17.2 %collective-permute-done.4 = bf16[4,64,1024]{2,1,0:T(8,128)(2,1)S(1)} collective-permute-done((bf16[4,64,1024]{2,1,0:T(8,128)(2,1)S(1)}, bf16[4,64,1024]{2,1,0:T(8,128)(2,1)S(1)}, u32[]{:S(2)}, u32[]{:S(2)}) %collective-permute-start.4) | collective-permute-done | bytes 524320 | tf_op jit(solution)/shard_map/ppermute | solution.py:12
  117.8 2.5 fusion.144
  123.2 2.4 broadcast_select_fusion.26
  126.7 6.3 %collective-permute-done.5 = bf16[4,64,1024]{2,1,0:T(8,128)(2,1)S(1)} collective-permute-done((bf16[4,64,1024]{2,1,0:T(8,128)(2,1)S(1)}, bf16[4,64,1024]{2,1,0:T(8,128)(2,1)S(1)}, u32[]{:S(2)}, u32[]{:S(2)}) %collective-permute-start.5) | collective-permute-done | bytes 524320 | tf_op jit(solution)/shard_map/ppermute | solution.py:12
  135.6 3.5 %fusion.147 = bf16[8,64,1024]{2,1,0:T(8,128)(2,1)} fusion(bf16[8,64,1024]{2,1,0:T(8,128)(2,1)S(1)} %broadcast_select_fusion.24, bf16[8,64,1024]{2,1,0:T(8,128)(2,1)} %broadcast_select_fusion.25, bf16[8,64,1024]{2,1,0:T(8,128)(2,1)S(1)} %copy-done.6, bf16[8,64,1024]{2,1,0:T(8,128)(2,1)} %broadcast_select_fusion.27, bf16[12,8,64,256]{3,2,1,0:T(8,128)(2,1)} %param.9), kind=kOutput, calls=%fused_computation.161 | convolution fusion | flops 285736960 | bytes 5505024 | tf_op jit(solution)/shard_map/nrk,nkb->nrb/dot_general | solution.py:28
  139.1 4.5 %all-to-all-start = ((bf16[8,64,1024]{2,1,0:T(8,128)(2,1)}), bf16[8,64,1024]{2,1,0:T(8,128)(2,1)S(1)}, u32[]{:S(2)}, u32[]{:S(2)}) async-start(bf16[8,64,1024]{2,1,0:T(8,128)(2,1)} %fusion.147), calls=%async_computation | async-start | bytes 2097152 | tf_op jit(solution)/shard_map/all_to_all | solution.py:33
  143.7 15.9 %all-to-all-done = bf16[8,64,1024]{2,1,0:T(8,128)(2,1)S(1)} async-done(((bf16[8,64,1024]{2,1,0:T(8,128)(2,1)}), bf16[8,64,1024]{2,1,0:T(8,128)(2,1)S(1)}, u32[]{:S(2)}, u32[]{:S(2)}) %all-to-all-start) | async-done | bytes 1048608 | tf_op jit(solution)/shard_map/all_to_all | solution.py:33
  162.5 2.4 broadcast_select_fusion.22
  166.0 7.2 %collective-permute-done.6 = bf16[4,64,1024]{2,1,0:T(8,128)(2,1)S(1)} collective-permute-done((bf16[4,64,1024]{2,1,0:T(8,128)(2,1)S(1)}, bf16[4,64,1024]{2,1,0:T(8,128)(2,1)S(1)}, u32[]{:S(2)}, u32[]{:S(2)}) %collective-permute-start.6) | collective-permute-done | bytes 524320 | tf_op jit(solution)/shard_map/ppermute | solution.py:12
  175.8 2.5 fusion.150
  178.3 2.2 collective-permute-start.7
  182.7 2.4 broadcast_select_fusion.18
  186.3 6.1 %collective-permute-done.7 = bf16[4,64,1024]{2,1,0:T(8,128)(2,1)S(1)} collective-permute-done((bf16[4,64,1024]{2,1,0:T(8,128)(2,1)S(1)}, bf16[4,64,1024]{2,1,0:T(8,128)(2,1)S(1)}, u32[]{:S(2)}, u32[]{:S(2)}) %collective-permute-start.7) | collective-permute-done | bytes 524320 | tf_op jit(solution)/shard_map/ppermute | solution.py:12
  195.0 2.5 fusion.153
  197.6 1.6 gather_fusion.33
  199.8 2.4 broadcast_select_fusion.14
  203.4 5.9 %collective-permute-done.8 = bf16[4,64,1024]{2,1,0:T(8,128)(2,1)S(1)} collective-permute-done((bf16[4,64,1024]{2,1,0:T(8,128)(2,1)S(1)}, bf16[4,64,1024]{2,1,0:T(8,128)(2,1)S(1)}, u32[]{:S(2)}, u32[]{:S(2)}) %collective-permute-start.8) | collective-permute-done | bytes 524320 | tf_op jit(solution)/shard_map/ppermute | solution.py:12
  211.8 2.5 fusion.156
  214.4 2.7 collective-permute-start.9
  219.3 2.4 broadcast_select_fusion.10
  222.9 14.7 %collective-permute-done.9 = bf16[4,64,1024]{2,1,0:T(8,128)(2,1)S(1)} collective-permute-done((bf16[4,64,1024]{2,1,0:T(8,128)(2,1)S(1)}, bf16[4,64,1024]{2,1,0:T(8,128)(2,1)S(1)}, u32[]{:S(2)}, u32[]{:S(2)}) %collective-permute-start.9) | collective-permute-done | bytes 524320 | tf_op jit(solution)/shard_map/ppermute | solution.py:12
  240.2 2.5 fusion.159
  242.7 3.6 %collective-permute-start.10 = (bf16[4,64,1024]{2,1,0:T(8,128)(2,1)S(1)}, bf16[4,64,1024]{2,1,0:T(8,128)(2,1)S(1)}, u32[]{:S(2)}, u32[]{:S(2)}) collective-permute-start(bf16[4,64,1024]{2,1,0:T(8,128)(2,1)S(1)} %slice.513), channel_id=1, source_target_pairs={{0,16},{1,17},{2,18},{3,19},{4,20},{5,21},{6,22},{7,23},{8,24},{9,... | collective-permute-start | bytes 1572872 | tf_op jit(solution)/shard_map/ppermute | solution.py:12
  248.4 2.4 broadcast_select_fusion.6
  252.0 18.9 %collective-permute-done.10 = bf16[4,64,1024]{2,1,0:T(8,128)(2,1)S(1)} collective-permute-done((bf16[4,64,1024]{2,1,0:T(8,128)(2,1)S(1)}, bf16[4,64,1024]{2,1,0:T(8,128)(2,1)S(1)}, u32[]{:S(2)}, u32[]{:S(2)}) %collective-permute-start.10) | collective-permute-done | bytes 524320 | tf_op jit(solution)/shard_map/ppermute | solution.py:12
  273.5 2.5 fusion.162
  278.8 2.4 broadcast_select_fusion.3
  282.4 7.6 %collective-permute-done.11 = bf16[4,64,1024]{2,1,0:T(8,128)(2,1)S(1)} collective-permute-done((bf16[4,64,1024]{2,1,0:T(8,128)(2,1)S(1)}, bf16[4,64,1024]{2,1,0:T(8,128)(2,1)S(1)}, u32[]{:S(2)}, u32[]{:S(2)}) %collective-permute-start.11) | collective-permute-done | bytes 524320 | tf_op jit(solution)/shard_map/ppermute | solution.py:12
  292.5 3.5 %fusion.165 = bf16[8,64,1024]{2,1,0:T(8,128)(2,1)} fusion(bf16[8,64,1024]{2,1,0:T(8,128)(2,1)S(1)} %broadcast_select_fusion, bf16[8,64,1024]{2,1,0:T(8,128)(2,1)} %broadcast_select_fusion.1, bf16[8,64,1024]{2,1,0:T(8,128)(2,1)} %broadcast_select_fusion.2, bf16[8,64,1024]{2,1,0:T(8,128)(2,1)S(1)} %copy-done.12, bf16[12,8,64,256]{3,2,1,0:T(8,128)(2,1)} %param.9), kind=kOutput, calls=%fused_computation.167 | convolution fusion | flops 285736960 | bytes 5505024 | tf_op jit(solution)/shard_map/nrk,nkb->nrb/dot_general | solution.py:28
  (228 shorter events, 75.2 us)
Async XLA Ops:
  0.0 13.1 %copy-start = (bf16[8,64,1024]{2,1,0:T(8,128)(2,1)S(1)}, bf16[8,64,1024]{2,1,0:T(8,128)(2,1)}, u32[]{:S(2)}) copy-start(bf16[8,64,1024]{2,1,0:T(8,128)(2,1)} %param.8) | copy-start | bytes 3145732
  1.2 13.8 %collective-permute-start = (bf16[4,64,1024]{2,1,0:T(8,128)(2,1)S(1)}, bf16[4,64,1024]{2,1,0:T(8,128)(2,1)S(1)}, u32[]{:S(2)}, u32[]{:S(2)}) collective-permute-start(bf16[4,64,1024]{2,1,0:T(8,128)(2,1)S(1)} %slice.338), channel_id=1, source_target_pairs={{0,1},{1,0},{2,3},{3,2},{4,5},{5,4},{6,7},{7,6},{8,9},{9,8},{10,11... | collective-permute-start | bytes 1572872 | tf_op jit(solution)/shard_map/ppermute | solution.py:12
  15.6 1.9 copy-start.1
  20.1 14.0 %collective-permute-start.1 = (bf16[4,64,1024]{2,1,0:T(8,128)(2,1)S(1)}, bf16[4,64,1024]{2,1,0:T(8,128)(2,1)S(1)}, u32[]{:S(2)}, u32[]{:S(2)}) collective-permute-start(bf16[4,64,1024]{2,1,0:T(8,128)(2,1)S(1)} %slice.504), channel_id=1, source_target_pairs={{0,2},{1,3},{2,0},{3,1},{4,6},{5,7},{6,4},{7,5},{8,10},{9,11},{10,... | collective-permute-start | bytes 1572872 | tf_op jit(solution)/shard_map/ppermute | solution.py:12
  34.7 1.9 copy-start.2
  39.2 12.4 %collective-permute-start.2 = (bf16[4,64,1024]{2,1,0:T(8,128)(2,1)S(1)}, bf16[4,64,1024]{2,1,0:T(8,128)(2,1)S(1)}, u32[]{:S(2)}, u32[]{:S(2)}) collective-permute-start(bf16[4,64,1024]{2,1,0:T(8,128)(2,1)S(1)} %slice.505), channel_id=1, source_target_pairs={{0,4},{1,5},{2,6},{3,7},{4,0},{5,1},{6,2},{7,3},{8,12},{9,13},{10,... | collective-permute-start | bytes 1572872 | tf_op jit(solution)/shard_map/ppermute | solution.py:12
  52.2 1.9 copy-start.3
  56.7 24.0 %collective-permute-start.3 = (bf16[4,64,1024]{2,1,0:T(8,128)(2,1)S(1)}, bf16[4,64,1024]{2,1,0:T(8,128)(2,1)S(1)}, u32[]{:S(2)}, u32[]{:S(2)}) collective-permute-start(bf16[4,64,1024]{2,1,0:T(8,128)(2,1)S(1)} %slice.506), channel_id=1, source_target_pairs={{0,8},{1,9},{2,10},{3,11},{4,12},{5,13},{6,14},{7,15},{8,0},{9,1},... | collective-permute-start | bytes 1572872 | tf_op jit(solution)/shard_map/ppermute | solution.py:12
  81.3 1.9 copy-start.4
  85.8 29.4 %collective-permute-start.4 = (bf16[4,64,1024]{2,1,0:T(8,128)(2,1)S(1)}, bf16[4,64,1024]{2,1,0:T(8,128)(2,1)S(1)}, u32[]{:S(2)}, u32[]{:S(2)}) collective-permute-start(bf16[4,64,1024]{2,1,0:T(8,128)(2,1)S(1)} %slice.507), channel_id=1, source_target_pairs={{0,16},{1,17},{2,18},{3,19},{4,20},{5,21},{6,22},{7,23},{8,24},{9,... | collective-permute-start | bytes 1572872 | tf_op jit(solution)/shard_map/ppermute | solution.py:12
  115.8 1.9 copy-start.5
  120.3 12.7 %collective-permute-start.5 = (bf16[4,64,1024]{2,1,0:T(8,128)(2,1)S(1)}, bf16[4,64,1024]{2,1,0:T(8,128)(2,1)S(1)}, u32[]{:S(2)}, u32[]{:S(2)}) collective-permute-start(bf16[4,64,1024]{2,1,0:T(8,128)(2,1)S(1)} %slice.508), channel_id=1, source_target_pairs={{0,1},{1,0},{2,3},{3,2},{4,5},{5,4},{6,7},{7,6},{8,9},{9,8},{10,11... | collective-permute-start | bytes 1572872 | tf_op jit(solution)/shard_map/ppermute | solution.py:12
  133.7 1.9 copy-start.6
  139.1 20.5 %all-to-all-start = ((bf16[8,64,1024]{2,1,0:T(8,128)(2,1)}), bf16[8,64,1024]{2,1,0:T(8,128)(2,1)S(1)}, u32[]{:S(2)}, u32[]{:S(2)}) async-start(bf16[8,64,1024]{2,1,0:T(8,128)(2,1)} %fusion.147), calls=%async_computation | async-start | bytes 2097152 | tf_op jit(solution)/shard_map/all_to_all | solution.py:33
  159.6 13.6 %collective-permute-start.6 = (bf16[4,64,1024]{2,1,0:T(8,128)(2,1)S(1)}, bf16[4,64,1024]{2,1,0:T(8,128)(2,1)S(1)}, u32[]{:S(2)}, u32[]{:S(2)}) collective-permute-start(bf16[4,64,1024]{2,1,0:T(8,128)(2,1)S(1)} %slice.509), channel_id=1, source_target_pairs={{0,1},{1,0},{2,3},{3,2},{4,5},{5,4},{6,7},{7,6},{8,9},{9,8},{10,11... | collective-permute-start | bytes 1572872 | tf_op jit(solution)/shard_map/ppermute | solution.py:12
  173.8 1.9 copy-start.7
  178.3 14.2 %collective-permute-start.7 = (bf16[4,64,1024]{2,1,0:T(8,128)(2,1)S(1)}, bf16[4,64,1024]{2,1,0:T(8,128)(2,1)S(1)}, u32[]{:S(2)}, u32[]{:S(2)}) collective-permute-start(bf16[4,64,1024]{2,1,0:T(8,128)(2,1)S(1)} %slice.510), channel_id=1, source_target_pairs={{0,2},{1,3},{2,0},{3,1},{4,6},{5,7},{6,4},{7,5},{8,10},{9,11},{10,... | collective-permute-start | bytes 1572872 | tf_op jit(solution)/shard_map/ppermute | solution.py:12
  193.1 1.9 copy-start.8
  197.5 11.7 %collective-permute-start.8 = (bf16[4,64,1024]{2,1,0:T(8,128)(2,1)S(1)}, bf16[4,64,1024]{2,1,0:T(8,128)(2,1)S(1)}, u32[]{:S(2)}, u32[]{:S(2)}) collective-permute-start(bf16[4,64,1024]{2,1,0:T(8,128)(2,1)S(1)} %slice.511), channel_id=1, source_target_pairs={{0,4},{1,5},{2,6},{3,7},{4,0},{5,1},{6,2},{7,3},{8,12},{9,13},{10,... | collective-permute-start | bytes 1572872 | tf_op jit(solution)/shard_map/ppermute | solution.py:12
  209.9 1.9 copy-start.9
  214.4 23.2 %collective-permute-start.9 = (bf16[4,64,1024]{2,1,0:T(8,128)(2,1)S(1)}, bf16[4,64,1024]{2,1,0:T(8,128)(2,1)S(1)}, u32[]{:S(2)}, u32[]{:S(2)}) collective-permute-start(bf16[4,64,1024]{2,1,0:T(8,128)(2,1)S(1)} %slice.512), channel_id=1, source_target_pairs={{0,8},{1,9},{2,10},{3,11},{4,12},{5,13},{6,14},{7,15},{8,0},{9,1},... | collective-permute-start | bytes 1572872 | tf_op jit(solution)/shard_map/ppermute | solution.py:12
  238.2 1.9 copy-start.10
  242.7 28.2 %collective-permute-start.10 = (bf16[4,64,1024]{2,1,0:T(8,128)(2,1)S(1)}, bf16[4,64,1024]{2,1,0:T(8,128)(2,1)S(1)}, u32[]{:S(2)}, u32[]{:S(2)}) collective-permute-start(bf16[4,64,1024]{2,1,0:T(8,128)(2,1)S(1)} %slice.513), channel_id=1, source_target_pairs={{0,16},{1,17},{2,18},{3,19},{4,20},{5,21},{6,22},{7,23},{8,24},{9,... | collective-permute-start | bytes 1572872 | tf_op jit(solution)/shard_map/ppermute | solution.py:12
  271.5 1.9 copy-start.11
  276.0 13.9 %collective-permute-start.11 = (bf16[4,64,1024]{2,1,0:T(8,128)(2,1)S(1)}, bf16[4,64,1024]{2,1,0:T(8,128)(2,1)S(1)}, u32[]{:S(2)}, u32[]{:S(2)}) collective-permute-start(bf16[4,64,1024]{2,1,0:T(8,128)(2,1)S(1)} %slice.514), channel_id=1, source_target_pairs={{0,1},{1,0},{2,3},{3,2},{4,5},{5,4},{6,7},{7,6},{8,9},{9,8},{10,11... | collective-permute-start | bytes 1572872 | tf_op jit(solution)/shard_map/ppermute | solution.py:12
  290.5 2.0 copy-start.12
where the time goes:
time: 297 us; the launch traced here: 296 us
  waiting for transfers between devices  125 us (42%)
  other arithmetic  57.9 us (19%)
  local copies, waits for them, and re-layouts  48.2 us (16%)
  matrix products  31.7 us (11%)
  starting transfers between devices  31.6 us (11%)
    ppermute x12, waiting for transfers between devices, swapped(): return lax.ppermute(value, axis, pairs)  109 us
    dot_general x12, matrix products, advance(): jnp.einsum('nrk,nkb->nrb', matrices, stacked, preferred_element_type=jnp....  31.7 us
    ppermute x12, starting transfers between devices, swapped(): return lax.ppermute(value, axis, pairs)  27.1 us
    select_n x24, other arithmetic, advance(): jnp.take(current, near_links[1], axis=0)  26.2 us
    gather x12, local copies, waits for them, and re-layouts, advance(): jnp.take(current, near_links[1], axis=0)  18.3 us
    all_to_all x1, waiting for transfers between devices, switch_groups(): lax.all_to_all(current, 'grp', split_axis=0, concat_axis=0, tiled=True)  15.9 us
    select_n x13, other arithmetic, advance(): jnp.take(current, near_links[0], axis=0)  15.5 us
    select_n x13, other arithmetic, advance(): jnp.take(partner_rows, far_links[0], axis=0)  13.6 us
  transfers between devices with their start and end apart: 13, of which 12 were waited for; matrix products, arithmetic and copies ran while one was open for 25% of the time, Pallas kernels for 0%

commit v1 on v0

v1 whole, which is shorter than its diff:
```python
import functools

import jax
import jax.numpy as jnp
from jax import lax
from jax.experimental import pallas as pl
from jax.experimental.pallas import tpu as pltpu
from jax.sharding import PartitionSpec as P

MESH = pl.DeviceIdType.MESH
SEND = 4
CHUNKS = 4
STEP_AT = (0.0, 4.0, 8.0, 12.0, 17.0, 23.0, 27.0, 31.0, 35.0, 39.0, 43.0, 48.0, 54.0)
STAGGER = 9.0
AHEAD = 2


def flipped(index, mask):
    return index + mask - 2 * mask * lax.rem(index // mask, 2)


def kernel(
    sizes, leaves, translate, near, far, out, z, w, tv, send, recv, sw_send, sw_recv, leaf_sem, tr_sem, out_sem
):
    levels, nodes, rank, cols, groups, box_bits = sizes
    half = levels // 2
    pre, last = levels, levels + 1
    q = lax.axis_index("grp")
    b = lax.axis_index("box")
    lead = SEND * rank
    depth = nodes * rank

    def partner(level):
        return (q, flipped(b, 1 << (level % half % box_bits)))

    def columns(s):
        return pl.ds(s * cols, cols)

    def out_place(level):
        return pre if level == half - 1 else last if level == levels - 1 else level + 1

    def exchange(level, s):
        if level == 0:
            src = leaves.at[pl.ds(0, SEND), :, columns(s)]
        else:
            src = z.at[level, s, pl.ds(0, SEND)]
        return pltpu.make_async_remote_copy(
            src,
            z.at[level, s, pl.ds(nodes, SEND)],
            send.at[level, s],
            recv.at[level, s],
            device_id=partner(level),
            device_id_type=MESH,
        )

    def switch(s, r):
        to = lax.rem(q + r, groups)
        return pltpu.make_async_remote_copy(
            z.at[pre, s, to],
            z.at[half, s, q],
            sw_send.at[s, r - 1],
            sw_recv.at[s, r - 1],
            device_id=(to, b),
            device_id_type=MESH,
        )

    def leaf_copy(s):
        return pltpu.make_async_copy(
            leaves.at[:, :, columns(s)], z.at[0, s, pl.ds(0, nodes)], leaf_sem.at[s]
        )

    def tr_copy(level):
        return pltpu.make_async_copy(translate.at[level], tv.at[level], tr_sem.at[level])

    def out_copy(s):
        return pltpu.make_async_copy(
            z.at[last, s, pl.ds(0, nodes)], out.at[:, :, columns(s)], out_sem.at[s]
        )

    lane = lax.broadcasted_iota(jnp.int32, (rank, 2 * rank), 1)
    left = lane < rank
    side = jnp.where(left, 0, 1)

    def build(level):
        tr_copy(level).wait()

        def one(n, carry):
            rows = pl.ds(pl.multiple_of(n * rank, rank), rank)
            for links, count, first in ((near, nodes, 0), (far, SEND, nodes)):
                pair = tv[level, n, :, pl.ds(0 if first == 0 else 2 * rank, 2 * rank)].astype(jnp.float32)
                turned = pltpu.roll(pair, rank, 1)
                one_link = links[level, 0, n]
                two_link = links[level, 1, n]
                at_pair = jnp.where(left, one_link, two_link) - side
                at_turned = jnp.where(left, two_link, one_link) - side
                for j in range(count // 2):
                    spread = jnp.where(at_pair == 2 * j, pair, 0.0) + jnp.where(at_turned == 2 * j, turned, 0.0)
                    w[level, rows, pl.ds((first + 2 * j) * rank, 2 * rank)] = spread.astype(w.dtype)
            return carry

        lax.fori_loop(0, nodes, one, 0)

    def product(level, s, first):
        stacked = z[level, s].reshape((nodes + SEND) * rank, cols)
        summed = jnp.dot(w[level, pl.ds(first * rank, lead), :], stacked, preferred_element_type=jnp.float32)
        z[out_place(level), s, pl.ds(first, SEND)] = summed.astype(z.dtype).reshape(SEND, rank, cols)

    def step(level, s):
        if level == 0:
            leaf_copy(s).wait()
        exchange(level, s).wait_recv()
        product(level, s, 0)
        if level + 1 < levels and level + 1 != half:
            exchange(level + 1, s).start()
        product(level, s, SEND)
        if level + 1 == half:
            for r in range(1, groups):
                switch(s, r).start()
            z[half, s, q] = z[pre, s, q]
        if level + 1 == levels:
            out_copy(s).start()

    def forward(s):
        for r in range(1, groups):
            switch(s, r).wait_recv()
        exchange(half, s).start()

    barrier = pltpu.get_barrier_semaphore()
    for bit in range(box_bits):
        pl.semaphore_signal(barrier, inc=1, device_id=partner(bit), device_id_type=MESH)
    for r in range(1, groups):
        pl.semaphore_signal(barrier, inc=1, device_id=(lax.rem(q + r, groups), b), device_id_type=MESH)
    for s in range(CHUNKS):
        leaf_copy(s).start()
        if s == 0:
            tr_copy(0).start()
    for level in range(1, levels):
        tr_copy(level).start()
    pl.semaphore_wait(barrier, box_bits + groups - 1)
    for s in range(min(AHEAD, CHUNKS)):
        exchange(0, s).start()
    build(0)

    tasks = sorted((STEP_AT[i] + STAGGER * s, i, s) for s in range(CHUNKS) for i in range(levels + 1))
    for _, i, s in tasks:
        if i == half:
            forward(s)
            continue
        level = i if i < half else i - 1
        step(level, s)
        if level == 0 and s + AHEAD < CHUNKS:
            exchange(0, s + AHEAD).start()
        if s == 0 and level + 1 < levels:
            build(level + 1)

    for s in range(CHUNKS):
        for level in range(levels):
            exchange(level, s).wait_send()
        for r in range(1, groups):
            switch(s, r).wait_send()
        out_copy(s).wait()


def on_device(leaves, translate, local_links, remote_links):
    nodes, rank, traces = leaves.shape
    levels = translate.shape[0]
    groups = lax.axis_size("grp")
    box_bits = lax.axis_size("box").bit_length() - 1
    cols = traces // CHUNKS
    width = nodes + SEND
    sizes = (levels, nodes, rank, cols, groups, box_bits)
    anywhere = pl.BlockSpec(memory_space=pl.ANY)
    scalars = pl.BlockSpec(memory_space=pltpu.SMEM)
    dma = pltpu.SemaphoreType.DMA
    return pl.pallas_call(
        functools.partial(kernel, sizes),
        out_shape=jax.ShapeDtypeStruct(leaves.shape, leaves.dtype),
        in_specs=[anywhere, anywhere, scalars, scalars],
        out_specs=anywhere,
        scratch_shapes=[
            pltpu.VMEM((levels + 2, CHUNKS, width, rank, cols), leaves.dtype),
            pltpu.VMEM((levels, nodes * rank, width * rank), leaves.dtype),
            pltpu.VMEM(translate.shape, translate.dtype),
            dma((levels, CHUNKS)),
            dma((levels, CHUNKS)),
            dma((CHUNKS, groups - 1)),
            dma((CHUNKS, groups - 1)),
            dma((CHUNKS,)),
            dma((levels,)),
            dma((CHUNKS,)),
        ],
        name="butterfly",
        compiler_params=pltpu.CompilerParams(
            collective_id=0, has_side_effects=True, vmem_limit_bytes=48 << 20
        ),
    )(leaves, translate, local_links, remote_links)


def solution(mesh):
    placed = (
        P(("grp", "box"), None, None),
        P(None, ("grp", "box"), None, None),
        P(None, None, ("grp", "box")),
        P(None, None, ("grp", "box")),
    )
    return jax.shard_map(
        on_device,
        mesh=mesh,
        in_specs=placed,
        out_specs=P(("grp", "box"), None, None),
        check_vma=False,
    )
```

time: 297 us -> 169 us (0.57)
  Pallas kernels: 0 us -> 163 us
  waiting for transfers between devices: 125 us -> 0 us
  other arithmetic: 57.9 us -> 0 us
  local copies, waits for them, and re-layouts: 48.2 us -> 5.65 us
  matrix products: 31.7 us -> 0 us
  starting transfers between devices: 31.6 us -> 0 us
    pallas_call x0 -> x1, Pallas kernels: none -> 163 us  [on_device(): pl.pallas_call(functools.partial(kernel, sizes), out_shape=jax.ShapeDtype...]
    ppermute x12 -> x0, waiting for transfers between devices: 109 us -> none  [swapped(): return lax.ppermute(value, axis, pairs)]
    select_n x74 -> x0, other arithmetic: 57.4 us -> none  [the longest x24 26.2 us: advance(): jnp.take(current, near_links[1], axis=0)]
    gather x48 -> x0, local copies, waits for them, and re-layouts: 41.3 us -> none  [the longest x12 18.3 us: advance(): jnp.take(current, near_links[1], axis=0)]
    dot_general x12 -> x0, matrix products: 31.7 us -> none  [advance(): jnp.einsum('nrk,nkb->nrb', matrices, stacked, preferred_element_type=jnp....]
    ppermute x12 -> x0, starting transfers between devices: 27.1 us -> none  [swapped(): return lax.ppermute(value, axis, pairs)]
    all_to_all x1 -> x0, waiting for transfers between devices: 15.9 us -> none  [switch_groups(): lax.all_to_all(current, 'grp', split_axis=0, concat_axis=0, tiled=True)]
    slice x16 -> x0, local copies, waits for them, and re-layouts: 6.84 us -> none  [the longest x1 1.59 us: advance(): far_links[0]]
  transfers between devices with their start and end apart: 13 -> 0, of which waited for: 12 -> 0; matrix products, arithmetic and copies ran while one was open for 25% -> 0% of each run, Pallas kernels for 0% -> 0%
where the time goes in v1:
time: 169 us; the launch traced here: 168 us
  Pallas kernels  163 us (96%)
  local copies, waits for them, and re-layouts  5.65 us (3%)
    pallas_call x1, Pallas kernels, on_device(): pl.pallas_call(functools.partial(kernel, sizes), out_shape=jax.ShapeDtype...  163 us
    unnamed x7, local copies, waits for them, and re-layouts  5.65 us

profile of v1, /device:TPU:2, one launch (start us, length us, event | category | flops | bytes accessed | tf_op | source)
XLA Modules:
  0.0 168.4 jit_solution(1712750049553851162)
XLA Ops:
  0.0 0.8 copy.5.near
  0.8 0.8 copy.6.far
  1.6 0.0 copy-start
  1.6 1.9 %copy-done = bf16[12,8,64,256]{3,2,1,0:T(8,128)(2,1)S(1)} copy-done((bf16[12,8,64,256]{3,2,1,0:T(8,128)(2,1)S(1)}, bf16[12,8,64,256]{3,2,1,0:T(8,128)(2,1)}, u32[]{:S(2)}) %copy-start) | copy-done | bytes 3145752
  3.5 0.0 copy-start.1
  3.5 1.2 copy-done.1
  4.7 162.8 %butterfly.1 = bf16[8,64,1024]{2,1,0:T(8,128)(2,1)S(1)} custom-call(bf16[8,64,1024]{2,1,0:T(8,128)(2,1)S(1)} %copy-done.1, bf16[12,8,64,256]{3,2,1,0:T(8,128)(2,1)S(1)} %copy-done, s32[12,2,8]{2,1,0:T(2,128)S(1)} %copy.5.near, s32[12,2,8]{2,1,0:T(2,128)S(1)} %copy.6.far), custom_call_target="tpu_custom_call" | custom-call | tf_op jit(solution)/shard_map/butterfly/pallas_call | solution.py:175
  167.5 1.0 copy.8
Async XLA Ops:
  1.6 1.9 %copy-start = (bf16[12,8,64,256]{3,2,1,0:T(8,128)(2,1)S(1)}, bf16[12,8,64,256]{3,2,1,0:T(8,128)(2,1)}, u32[]{:S(2)}) copy-start(bf16[12,8,64,256]{3,2,1,0:T(8,128)(2,1)} %translate.1) | copy-start | bytes 9437188
  3.5 1.2 copy-start.1

commit v2 on v1

--- a/solution.py
+++ b/solution.py
@@ -9,10 +9,9 @@
 
 MESH = pl.DeviceIdType.MESH
 SEND = 4
-CHUNKS = 4
-STEP_AT = (0.0, 4.0, 8.0, 12.0, 17.0, 23.0, 27.0, 31.0, 35.0, 39.0, 43.0, 48.0, 54.0)
-STAGGER = 9.0
-AHEAD = 2
+CHUNKS = 8
+BUILD = 8
+ORDER = 0xf4808544008744185500744170365205844757513828320014477152354460012170640742325815464177360350257271140564063851717304045587712686251307307421243371576630032621515673327661331025656223314461576722303662581127036631225466326
 
 
 def flipped(index, mask):
@@ -20,7 +19,7 @@
 
 
 def kernel(
-    sizes, leaves, translate, near, far, out, z, w, tv, send, recv, sw_send, sw_recv, leaf_sem, tr_sem, out_sem
+    sizes, leaves, translate, near_in, far_in, out, z, w, tv, near, far, link_sem, send, recv, sw_send, sw_recv, leaf_sem, tr_sem, out_sem
 ):
     levels, nodes, rank, cols, groups, box_bits = sizes
     half = levels // 2
@@ -77,6 +76,12 @@
             z.at[last, s, pl.ds(0, nodes)], out.at[:, :, columns(s)], out_sem.at[s]
         )
 
+    def link_copies():
+        return [
+            pltpu.make_async_copy(src, dst, link_sem.at[i])
+            for i, (src, dst) in enumerate(((near_in, near), (far_in, far)))
+        ]
+
     lane = lax.broadcasted_iota(jnp.int32, (rank, 2 * rank), 1)
     left = lane < rank
     side = jnp.where(left, 0, 1)
@@ -89,8 +94,8 @@
             for links, count, first in ((near, nodes, 0), (far, SEND, nodes)):
                 pair = tv[level, n, :, pl.ds(0 if first == 0 else 2 * rank, 2 * rank)].astype(jnp.float32)
                 turned = pltpu.roll(pair, rank, 1)
-                one_link = links[level, 0, n]
-                two_link = links[level, 1, n]
+                one_link = links[0, n, level]
+                two_link = links[1, n, level]
                 at_pair = jnp.where(left, one_link, two_link) - side
                 at_turned = jnp.where(left, two_link, one_link) - side
                 for j in range(count // 2):
@@ -105,26 +110,21 @@
         summed = jnp.dot(w[level, pl.ds(first * rank, lead), :], stacked, preferred_element_type=jnp.float32)
         z[out_place(level), s, pl.ds(first, SEND)] = summed.astype(z.dtype).reshape(SEND, rank, cols)
 
-    def step(level, s):
+    def step(level, s, then):
         if level == 0:
             leaf_copy(s).wait()
         exchange(level, s).wait_recv()
         product(level, s, 0)
-        if level + 1 < levels and level + 1 != half:
-            exchange(level + 1, s).start()
+        if then is not None:
+            then()
         product(level, s, SEND)
         if level + 1 == half:
-            for r in range(1, groups):
-                switch(s, r).start()
             z[half, s, q] = z[pre, s, q]
         if level + 1 == levels:
             out_copy(s).start()
 
-    def forward(s):
-        for r in range(1, groups):
-            switch(s, r).wait_recv()
-        exchange(half, s).start()
-
+    for copy in link_copies():
+        copy.start()
     barrier = pltpu.get_barrier_semaphore()
     for bit in range(box_bits):
         pl.semaphore_signal(barrier, inc=1, device_id=partner(bit), device_id_type=MESH)
@@ -137,21 +137,41 @@
     for level in range(1, levels):
         tr_copy(level).start()
     pl.semaphore_wait(barrier, box_bits + groups - 1)
-    for s in range(min(AHEAD, CHUNKS)):
-        exchange(0, s).start()
-    build(0)
-
-    tasks = sorted((STEP_AT[i] + STAGGER * s, i, s) for s in range(CHUNKS) for i in range(levels + 1))
-    for _, i, s in tasks:
+    for copy in link_copies():
+        copy.wait()
+
+    def level_of(i):
+        return i if i < half else i - 1
+
+    def begin(i, s):
         if i == half:
-            forward(s)
+            for r in range(1, groups):
+                switch(s, r).start()
+        else:
+            exchange(level_of(i), s).start()
+
+    order = [int(digit) for digit in f"{ORDER:x}"[1:]]
+    at = [0] * CHUNKS
+    built = 0
+    while order:
+        s = order.pop(0)
+        if s == BUILD:
+            build(built)
+            built += 1
             continue
-        level = i if i < half else i - 1
-        step(level, s)
-        if level == 0 and s + AHEAD < CHUNKS:
-            exchange(0, s + AHEAD).start()
-        if s == 0 and level + 1 < levels:
-            build(level + 1)
+        i, working = divmod(at[s], 2)
+        at[s] += 1
+        if not working:
+            begin(i, s)
+        elif i == half:
+            for r in range(1, groups):
+                switch(s, r).wait_recv()
+        else:
+            early = i + 1 != half and order[:1] == [s]
+            if early:
+                order.pop(0)
+                at[s] += 1
+            step(level_of(i), s, functools.partial(begin, i + 1, s) if early else None)
 
     for s in range(CHUNKS):
         for level in range(levels):
@@ -170,17 +190,19 @@
     width = nodes + SEND
     sizes = (levels, nodes, rank, cols, groups, box_bits)
     anywhere = pl.BlockSpec(memory_space=pl.ANY)
-    scalars = pl.BlockSpec(memory_space=pltpu.SMEM)
     dma = pltpu.SemaphoreType.DMA
     return pl.pallas_call(
         functools.partial(kernel, sizes),
         out_shape=jax.ShapeDtypeStruct(leaves.shape, leaves.dtype),
-        in_specs=[anywhere, anywhere, scalars, scalars],
+        in_specs=[anywhere] * 4,
         out_specs=anywhere,
         scratch_shapes=[
             pltpu.VMEM((levels + 2, CHUNKS, width, rank, cols), leaves.dtype),
             pltpu.VMEM((levels, nodes * rank, width * rank), leaves.dtype),
             pltpu.VMEM(translate.shape, translate.dtype),
+            pltpu.SMEM((2, nodes, levels), local_links.dtype),
+            pltpu.SMEM((2, nodes, levels), remote_links.dtype),
+            dma((2,)),
             dma((levels, CHUNKS)),
             dma((levels, CHUNKS)),
             dma((CHUNKS, groups - 1)),
@@ -191,9 +213,9 @@
         ],
         name="butterfly",
         compiler_params=pltpu.CompilerParams(
-            collective_id=0, has_side_effects=True, vmem_limit_bytes=48 << 20
+            collective_id=0, has_side_effects=True, vmem_limit_bytes=49 << 20
         ),
-    )(leaves, translate, local_links, remote_links)
+    )(leaves, translate, local_links.transpose(1, 2, 0), remote_links.transpose(1, 2, 0))
 
 
 def solution(mesh):

time: 169 us -> 134 us (0.79)
  Pallas kernels: 163 us -> 130 us
  local copies, waits for them, and re-layouts: 5.65 us -> 3.59 us
    pallas_call x1, Pallas kernels: 163 us -> 130 us  [on_device(): pl.pallas_call(functools.partial(kernel, sizes), out_shape=jax.ShapeDtype...]
    unnamed x7, local copies, waits for them, and re-layouts: 5.65 us -> 3.59 us
where the time goes in v2:
time: 134 us; the launch traced here: 133 us
  Pallas kernels  130 us (97%)
  local copies, waits for them, and re-layouts  3.59 us (3%)
    pallas_call x1, Pallas kernels, on_device(): pl.pallas_call(functools.partial(kernel, sizes), out_shape=jax.ShapeDtype...  130 us
    unnamed x7, local copies, waits for them, and re-layouts  3.59 us

profile of v2, /device:TPU:2, one launch (start us, length us, event | category | flops | bytes accessed | tf_op | source)
XLA Modules:
  0.0 133.2 jit_solution(15600670509056371133)
XLA Ops:
  0.0 0.0 copy-start
  0.0 1.2 copy-done
  1.2 0.0 copy-start.1
  1.2 0.7 copy-done.1
  1.9 0.0 copy-start.2
  1.9 0.7 copy-done.2
  2.6 129.6 %butterfly.1 = bf16[8,64,1024]{2,1,0:T(8,128)(2,1)S(1)} custom-call(bf16[8,64,1024]{2,1,0:T(8,128)(2,1)S(1)} %copy-done, bf16[12,8,64,256]{3,2,1,0:T(8,128)(2,1)} %translate.1, s32[2,8,12]{2,1,0:T(8,128)S(1)} %bitcast.2, s32[2,8,12]{2,1,0:T(8,128)S(1)} %bitcast.3), custom_call_target="tpu_custom_call" | custom-call | tf_op jit(solution)/shard_map/butterfly/pallas_call | solution.py:194
  132.2 1.0 copy.6
Async XLA Ops:
  0.0 1.2 copy-start
  1.2 0.7 copy-start.1
  1.9 0.7 copy-start.2

commit v3 on v2

--- a/solution.py
+++ b/solution.py
@@ -11,6 +11,7 @@
 SEND = 4
 CHUNKS = 8
 BUILD = 8
+READ_AHEAD = 2
 ORDER = 0xf4808544008744185500744170365205844757513828320014477152354460012170640742325815464177360350257271140564063851717304045587712686251307307421243371576630032621515673327661331025656223314461576722303662581127036631225466326
 
 
@@ -87,7 +88,12 @@
     side = jnp.where(left, 0, 1)
 
     def build(level):
+        if level == 0:
+            for copy in link_copies():
+                copy.wait()
         tr_copy(level).wait()
+        if level + READ_AHEAD < levels:
+            tr_copy(level + READ_AHEAD).start()
 
         def one(n, carry):
             rows = pl.ds(pl.multiple_of(n * rank, rank), rank)
@@ -123,22 +129,16 @@
         if level + 1 == levels:
             out_copy(s).start()
 
-    for copy in link_copies():
-        copy.start()
     barrier = pltpu.get_barrier_semaphore()
     for bit in range(box_bits):
         pl.semaphore_signal(barrier, inc=1, device_id=partner(bit), device_id_type=MESH)
     for r in range(1, groups):
         pl.semaphore_signal(barrier, inc=1, device_id=(lax.rem(q + r, groups), b), device_id_type=MESH)
-    for s in range(CHUNKS):
-        leaf_copy(s).start()
-        if s == 0:
-            tr_copy(0).start()
-    for level in range(1, levels):
+    for copy in link_copies():
+        copy.start()
+    for level in range(READ_AHEAD):
         tr_copy(level).start()
     pl.semaphore_wait(barrier, box_bits + groups - 1)
-    for copy in link_copies():
-        copy.wait()
 
     def level_of(i):
         return i if i < half else i - 1
@@ -149,6 +149,8 @@
                 switch(s, r).start()
         else:
             exchange(level_of(i), s).start()
+        if i == 0:
+            leaf_copy(s).start()
 
     order = [int(digit) for digit in f"{ORDER:x}"[1:]]
     at = [0] * CHUNKS
@@ -213,7 +215,7 @@
         ],
         name="butterfly",
         compiler_params=pltpu.CompilerParams(
-            collective_id=0, has_side_effects=True, vmem_limit_bytes=49 << 20
+            collective_id=0, has_side_effects=True, vmem_limit_bytes=60 << 20
         ),
     )(leaves, translate, local_links.transpose(1, 2, 0), remote_links.transpose(1, 2, 0))
 

time: 134 us -> 133 us (level)
    unnamed x7 -> x1, local copies, waits for them, and re-layouts: 3.59 us -> 2.26 us
where the time goes in v3:
time: 133 us
  Pallas kernels  130 us (98%)
  local copies, waits for them, and re-layouts  2.26 us (2%)
    pallas_call x1, Pallas kernels, on_device(): pl.pallas_call(functools.partial(kernel, sizes), out_shape=jax.ShapeDtype...  130 us

profile of v3, /device:TPU:2, one launch (start us, length us, event | category | flops | bytes accessed | tf_op | source)
XLA Modules:
  0.0 132.7 jit_solution(7767035047249139231)
XLA Ops:
  0.0 130.4 %butterfly.1 = bf16[8,64,1024]{2,1,0:T(8,128)(2,1)} custom-call(bf16[8,64,1024]{2,1,0:T(8,128)(2,1)} %leaves.1, bf16[12,8,64,256]{3,2,1,0:T(8,128)(2,1)} %translate.1, s32[2,8,12]{2,1,0:T(8,128)} %bitcast.2, s32[2,8,12]{2,1,0:T(8,128)} %bitcast.3), custom_call_target="tpu_custom_call" | custom-call | tf_op jit(solution)/shard_map/butterfly/pallas_call | solution.py:196
  130.4 2.3 %copy.6 = bf16[8,64,1024]{2,1,0:T(8,128)(2,1)} copy(bf16[8,64,1024]{2,1,0:T(8,128)(2,1)} %butterfly.1) | data formatting | bytes 2097152

commit v4 on v3

--- a/solution.py
+++ b/solution.py
@@ -20,11 +20,11 @@
 
 
 def kernel(
-    sizes, leaves, translate, near_in, far_in, out, z, w, tv, near, far, link_sem, send, recv, sw_send, sw_recv, leaf_sem, tr_sem, out_sem
+    sizes, leaves, translate, links_in, out, z, w, tv, links, link_sem, send, recv, sw_send, sw_recv, leaf_sem, tr_sem
 ):
     levels, nodes, rank, cols, groups, box_bits = sizes
     half = levels // 2
-    pre, last = levels, levels + 1
+    pre = levels
     q = lax.axis_index("grp")
     b = lax.axis_index("box")
     lead = SEND * rank
@@ -37,7 +37,7 @@
         return pl.ds(s * cols, cols)
 
     def out_place(level):
-        return pre if level == half - 1 else last if level == levels - 1 else level + 1
+        return pre if level == half - 1 else level + 1
 
     def exchange(level, s):
         if level == 0:
@@ -72,16 +72,7 @@
     def tr_copy(level):
         return pltpu.make_async_copy(translate.at[level], tv.at[level], tr_sem.at[level])
 
-    def out_copy(s):
-        return pltpu.make_async_copy(
-            z.at[last, s, pl.ds(0, nodes)], out.at[:, :, columns(s)], out_sem.at[s]
-        )
-
-    def link_copies():
-        return [
-            pltpu.make_async_copy(src, dst, link_sem.at[i])
-            for i, (src, dst) in enumerate(((near_in, near), (far_in, far)))
-        ]
+    link_copy = pltpu.make_async_copy(links_in, links, link_sem)
 
     lane = lax.broadcasted_iota(jnp.int32, (rank, 2 * rank), 1)
     left = lane < rank
@@ -89,19 +80,18 @@
 
     def build(level):
         if level == 0:
-            for copy in link_copies():
-                copy.wait()
+            link_copy.wait()
         tr_copy(level).wait()
         if level + READ_AHEAD < levels:
             tr_copy(level + READ_AHEAD).start()
 
         def one(n, carry):
             rows = pl.ds(pl.multiple_of(n * rank, rank), rank)
-            for links, count, first in ((near, nodes, 0), (far, SEND, nodes)):
+            for kind, count, first in ((0, nodes, 0), (1, SEND, nodes)):
                 pair = tv[level, n, :, pl.ds(0 if first == 0 else 2 * rank, 2 * rank)].astype(jnp.float32)
                 turned = pltpu.roll(pair, rank, 1)
-                one_link = links[0, n, level]
-                two_link = links[1, n, level]
+                one_link = links[kind, 0, n, level]
+                two_link = links[kind, 1, n, level]
                 at_pair = jnp.where(left, one_link, two_link) - side
                 at_turned = jnp.where(left, two_link, one_link) - side
                 for j in range(count // 2):
@@ -114,7 +104,11 @@
     def product(level, s, first):
         stacked = z[level, s].reshape((nodes + SEND) * rank, cols)
         summed = jnp.dot(w[level, pl.ds(first * rank, lead), :], stacked, preferred_element_type=jnp.float32)
-        z[out_place(level), s, pl.ds(first, SEND)] = summed.astype(z.dtype).reshape(SEND, rank, cols)
+        made = summed.astype(z.dtype).reshape(SEND, rank, cols)
+        if level + 1 == levels:
+            out[pl.ds(first, SEND), :, columns(s)] = made
+        else:
+            z[out_place(level), s, pl.ds(first, SEND)] = made
 
     def step(level, s, then):
         if level == 0:
@@ -126,16 +120,13 @@
         product(level, s, SEND)
         if level + 1 == half:
             z[half, s, q] = z[pre, s, q]
-        if level + 1 == levels:
-            out_copy(s).start()
 
     barrier = pltpu.get_barrier_semaphore()
     for bit in range(box_bits):
         pl.semaphore_signal(barrier, inc=1, device_id=partner(bit), device_id_type=MESH)
     for r in range(1, groups):
         pl.semaphore_signal(barrier, inc=1, device_id=(lax.rem(q + r, groups), b), device_id_type=MESH)
-    for copy in link_copies():
-        copy.start()
+    link_copy.start()
     for level in range(READ_AHEAD):
         tr_copy(level).start()
     pl.semaphore_wait(barrier, box_bits + groups - 1)
@@ -180,7 +171,6 @@
             exchange(level, s).wait_send()
         for r in range(1, groups):
             switch(s, r).wait_send()
-        out_copy(s).wait()
 
 
 def on_device(leaves, translate, local_links, remote_links):
@@ -196,28 +186,26 @@
     return pl.pallas_call(
         functools.partial(kernel, sizes),
         out_shape=jax.ShapeDtypeStruct(leaves.shape, leaves.dtype),
-        in_specs=[anywhere] * 4,
-        out_specs=anywhere,
+        in_specs=[anywhere] * 3,
+        out_specs=pl.BlockSpec(memory_space=pltpu.VMEM),
         scratch_shapes=[
-            pltpu.VMEM((levels + 2, CHUNKS, width, rank, cols), leaves.dtype),
+            pltpu.VMEM((levels + 1, CHUNKS, width, rank, cols), leaves.dtype),
             pltpu.VMEM((levels, nodes * rank, width * rank), leaves.dtype),
             pltpu.VMEM(translate.shape, translate.dtype),
-            pltpu.SMEM((2, nodes, levels), local_links.dtype),
-            pltpu.SMEM((2, nodes, levels), remote_links.dtype),
-            dma((2,)),
+            pltpu.SMEM((2, 2, nodes, levels), local_links.dtype),
+            dma,
             dma((levels, CHUNKS)),
             dma((levels, CHUNKS)),
             dma((CHUNKS, groups - 1)),
             dma((CHUNKS, groups - 1)),
             dma((CHUNKS,)),
             dma((levels,)),
-            dma((CHUNKS,)),
         ],
         name="butterfly",
         compiler_params=pltpu.CompilerParams(
-            collective_id=0, has_side_effects=True, vmem_limit_bytes=60 << 20
+            collective_id=0, has_side_effects=True, vmem_limit_bytes=52 << 20
         ),
-    )(leaves, translate, local_links.transpose(1, 2, 0), remote_links.transpose(1, 2, 0))
+    )(leaves, translate, jnp.stack([local_links, remote_links]).transpose(0, 2, 3, 1))
 
 
 def solution(mesh):

time: 133 us -> 133 us (level)
  no operation moved by 1% of the time
where the time goes in v4:
time: 133 us
  Pallas kernels  131 us (98%)
    pallas_call x1, Pallas kernels, on_device(): pl.pallas_call(functools.partial(kernel, sizes), out_shape=jax.ShapeDtype...  131 us

profile of v4, /device:TPU:2, one launch (start us, length us, event | category | flops | bytes accessed | tf_op | source)
XLA Modules:
  0.0 132.8 jit_solution(1563115375511450064)
XLA Ops:
  0.0 0.7 add_bitcast_fusion.links_in
  0.7 131.1 %butterfly.1 = bf16[8,64,1024]{2,1,0:T(8,128)(2,1)S(1)} custom-call(bf16[8,64,1024]{2,1,0:T(8,128)(2,1)} %leaves.1, bf16[12,8,64,256]{3,2,1,0:T(8,128)(2,1)} %translate.1, s32[2,2,8,12]{3,2,1,0:T(8,128)S(1)} %add_bitcast_fusion.links_in), custom_call_target="tpu_custom_call" | custom-call | tf_op jit(solution)/shard_map/butterfly/pallas_call | solution.py:186
  131.8 1.0 copy.6
